TPU v7x, 32 devices: a whole 2x2x4 slice. The times are simulated.
32 devices in a mesh: grp: 2 (over x), obs: 16 (over z, y, core).
Axes of the slice: x: 2, y: 2, z: 4, core: 2. Of those that a mesh axis runs over, the one named last changes fastest.
Arguments:
- anomalies: bfloat16 [512, 16384], P(('grp', 'obs')), parts along dimension 0, may hold values from -6 to 6
- innovations: bfloat16 [512, 16384], P(('grp', 'obs')), parts along dimension 0, may hold values from -6 to 6
- sort_order: int32 [32768], P(('grp', 'obs')), parts along dimension 0, may hold values from 0 to 16383, as said below
- obs_error: float32 [32768], P(('grp', 'obs')), parts along dimension 0, may hold values from 0.2 to 2
Outputs:
- gain_product: float32 [32768, 256], P(('grp', 'obs')), parts along dimension 0
There are 2 independent parts, one for each index of `grp`. A program takes and returns all parts, laid end to end along the dimension named above; each array names one. Nothing has to cross between parts.
Inputs may be any that keep to these rules, and one draw needn't show every extreme that they name: Each acquisition index appears exactly once, and sort_order[p] lies in the same aligned block of 128 positions as p.
All inputs are finite; a program needn't handle non-finite values.
Results may differ from a plain program's by a relative error of at most 0.0025.
Values may be sent and summed in bfloat16 or wider, within the bound.
A program may use at most 64 MiB of HBM per device.

v0:
```python
import jax
import jax.numpy as jnp
from jax import lax
from jax.sharding import PartitionSpec as P


def shifted(shard, axis, by):
    peers = lax.axis_size(axis)
    pairs = [(i, i + by) for i in range(peers) if 0 <= i + by < peers]
    return lax.ppermute(shard, axis, pairs)


def gaspari(z):
    inner = z * z * (z * (z * (-0.25 * z + 0.5) + 0.625) - 5.0 / 3.0) + 1.0
    zs = jnp.maximum(z, 1.0)
    outer = (
        zs * zs * (zs * (zs * (zs / 12.0 - 0.5) + 0.625) + 5.0 / 3.0)
        - 5.0 * zs
        + 4.0
        - 2.0 / (3.0 * zs)
    )
    return jnp.where(z <= 1.0, inner, jnp.where(z < 2.0, outer, 0.0 * z))


def taper_scale(first_row, rows, cols, offset, half_width, members):
    row_ids = first_row + lax.iota(jnp.int32, rows)
    col_ids = lax.iota(jnp.int32, cols) + offset * cols
    dist = jnp.abs(row_ids[:, None] - col_ids[None, :]).astype(jnp.float32)
    return gaspari(dist / half_width) / (members - 1.0)


def permute_blocks(values, selector, width, blocks):
    shaped = values.reshape(values.shape[0], blocks, width)
    moved = jnp.einsum("mbi,bij->mbj", shaped, selector, preferred_element_type=jnp.float32)
    return moved.astype(jnp.bfloat16).reshape(values.shape[0], blocks * width)


def on_device(anomalies, innovations, sort_order, obs_error):
    raw_y, raw_d = (
        lax.all_to_all(anomalies, "obs", split_axis=1, concat_axis=0, tiled=True),
        lax.all_to_all(innovations, "obs", split_axis=1, concat_axis=0, tiled=True),
    )
    members = raw_y.shape[0]
    panel = raw_y.shape[1]
    width = min(128, panel)
    blocks = panel // width
    local_ids = (sort_order % width).reshape(blocks, width)
    selector = (lax.iota(jnp.int32, width)[None, :, None] == local_ids[:, None, :]).astype(
        jnp.bfloat16
    )
    y_here = permute_blocks(raw_y, selector, width, blocks)
    d_here = permute_blocks(raw_d, selector, width, blocks)
    block = min(512, panel)
    half_width = panel // 2 * 1.0

    def tile_rows(first, y_cols, offset):
        row_part = lax.slice_in_dim(y_here, first, first + block, axis=1)
        gram = lax.dot_general(
            row_part, y_cols, (((0,), (0,)), ((), ())), preferred_element_type=jnp.float32
        )
        return (gram * taper_scale(first, block, panel, offset, half_width, members * 1.0)).astype(
            jnp.bfloat16
        )

    def apply_rows(weights, d_cols):
        return lax.dot_general(
            weights, d_cols, (((1,), (1,)), ((), ())), preferred_element_type=jnp.float32
        )

    pieces = []
    low_y, low_d = shifted((y_here, d_here), "obs", 1)
    up_y, up_d = shifted((y_here, d_here), "obs", -1)
    for first in range(0, panel, block):
        acc = apply_rows(tile_rows(first, y_here, 0), d_here)
        acc = acc + apply_rows(tile_rows(first, low_y, -1), low_d)
        acc = acc + apply_rows(tile_rows(first, up_y, 1), up_d)
        pieces.append(acc)
    total = jnp.concatenate(pieces, axis=0)
    return total + obs_error[:, None] * d_here.T.astype(jnp.float32)


def solution(mesh):
    return jax.shard_map(
        on_device,
        mesh=mesh,
        in_specs=(
            P(("grp", "obs"), None),
            P(("grp", "obs"), None),
            P(("grp", "obs")),
            P(("grp", "obs")),
        ),
        out_specs=P(("grp", "obs"), None),
        check_vma=False,
    )
```

profile of v0, /device:TPU:1, one launch (start us, length us, event | category | flops | bytes accessed | tf_op | source)
XLA Modules:
  0.0 76.1 jit_solution(12527095984979136979)
XLA Ops:
  0.0 1.9 %copy.19 = bf16[2,16,8,1024]{3,2,0,1:T(8,128)(2,1)} copy(bf16[2,16,8,1024]{3,2,1,0:T(8,128)(2,1)} %bitcast.47) | data formatting | bytes 1048576 | tf_op jit(solution)/shard_map/all_to_all | solution.py:41
  1.9 7.3 %all-to-all-start.1 = ((bf16[16,16,1024]{2,0,1:T(8,128)(2,1)}), bf16[16,16,1024]{2,0,1:T(8,128)(2,1)S(1)}, u32[]{:S(2)}, u32[]{:S(2)}) async-start(bf16[16,16,1024]{2,0,1:T(8,128)(2,1)} %bitcast.37), calls=%async_computation.1 | async-start | bytes 1048576 | tf_op jit(solution)/shard_map/all_to_all | solution.py:41
  9.3 0.0 copy-start.2
  9.3 0.8 %copy.20 = bf16[2,16,8,1024]{3,2,0,1:T(8,128)(2,1)} copy(bf16[2,16,8,1024]{3,2,1,0:T(8,128)(2,1)S(1)} %bitcast.48) | data formatting | bytes 1048576 | tf_op jit(solution)/shard_map/all_to_all | solution.py:40
  10.1 13.2 %all-to-all-done.1 = bf16[16,16,1024]{2,0,1:T(8,128)(2,1)S(1)} async-done(((bf16[16,16,1024]{2,0,1:T(8,128)(2,1)}), bf16[16,16,1024]{2,0,1:T(8,128)(2,1)S(1)}, u32[]{:S(2)}, u32[]{:S(2)}) %all-to-all-start.1) | async-done | bytes 524320 | tf_op jit(solution)/shard_map/all_to_all | solution.py:41
  23.4 4.5 %all-to-all-start = ((bf16[16,16,1024]{2,0,1:T(8,128)(2,1)}), bf16[16,16,1024]{2,0,1:T(8,128)(2,1)S(1)}, u32[]{:S(2)}, u32[]{:S(2)}) async-start(bf16[16,16,1024]{2,0,1:T(8,128)(2,1)} %bitcast.38), calls=%async_computation | async-start | bytes 1048576 | tf_op jit(solution)/shard_map/all_to_all | solution.py:40
  27.9 0.1 copy.12
  28.0 0.3 convolution_convert_fusion
  28.4 3.5 %collective-permute-start.1 = (bf16[256,1024]{0,1:T(8,128)(2,1)S(1)}, bf16[256,1024]{0,1:T(8,128)(2,1)S(1)}, u32[]{:S(2)}, u32[]{:S(2)}) collective-permute-start(bf16[256,1024]{0,1:T(8,128)(2,1)S(1)} %bitcast.39), channel_id=1, source_target_pairs={{0,1},{1,2},{2,3},{3,4},{4,5},{5,6},{6,7},{7,8},{8,9},{9,10},{10,1... | collective-permute-start | bytes 1572872 | tf_op jit(solution)/shard_map/ppermute | solution.py:10
  31.9 1.9 %collective-permute-start.3 = (bf16[256,1024]{0,1:T(8,128)(2,1)S(1)}, bf16[256,1024]{0,1:T(8,128)(2,1)S(1)}, u32[]{:S(2)}, u32[]{:S(2)}) collective-permute-start(bf16[256,1024]{0,1:T(8,128)(2,1)S(1)} %bitcast.40), channel_id=1, source_target_pairs={{1,0},{2,1},{3,2},{4,3},{5,4},{6,5},{7,6},{8,7},{9,8},{10,9},{11,1... | collective-permute-start | bytes 1572872 | tf_op jit(solution)/shard_map/ppermute | solution.py:10
  33.8 8.1 %all-to-all-done = bf16[16,16,1024]{2,0,1:T(8,128)(2,1)S(1)} async-done(((bf16[16,16,1024]{2,0,1:T(8,128)(2,1)}), bf16[16,16,1024]{2,0,1:T(8,128)(2,1)S(1)}, u32[]{:S(2)}, u32[]{:S(2)}) %all-to-all-start) | async-done | bytes 524320 | tf_op jit(solution)/shard_map/all_to_all | solution.py:40
  41.9 0.1 copy.11
  42.0 0.3 convolution_convert_fusion.1
  42.4 2.5 %collective-permute-start = (bf16[256,1024]{0,1:T(8,128)(2,1)S(1)}, bf16[256,1024]{0,1:T(8,128)(2,1)S(1)}, u32[]{:S(2)}, u32[]{:S(2)}) collective-permute-start(bf16[256,1024]{0,1:T(8,128)(2,1)S(1)} %bitcast.49), channel_id=1, source_target_pairs={{0,1},{1,2},{2,3},{3,4},{4,5},{5,6},{6,7},{7,8},{8,9},{9,10},{10,1... | collective-permute-start | bytes 1572872 | tf_op jit(solution)/shard_map/ppermute | solution.py:10
  44.9 1.9 %collective-permute-start.2 = (bf16[256,1024]{0,1:T(8,128)(2,1)S(1)}, bf16[256,1024]{0,1:T(8,128)(2,1)}, u32[]{:S(2)}, u32[]{:S(2)}) collective-permute-start(bf16[256,1024]{0,1:T(8,128)(2,1)S(1)} %bitcast.50), channel_id=1, source_target_pairs={{1,0},{2,1},{3,2},{4,3},{5,4},{6,5},{7,6},{8,7},{9,8},{10,9},{11,1... | collective-permute-start | bytes 1572872 | tf_op jit(solution)/shard_map/ppermute | solution.py:10
  46.8 3.8 %fusion.7 = f32[512,256]{1,0:T(8,128)} fusion(bf16[256,1024]{0,1:T(8,128)(2,1)S(1)} %bitcast.41, bf16[256,1024]{0,1:T(8,128)(2,1)S(1)} %bitcast.51, s32[512]{0:T(512)S(1)} %iota_add_fusion.2), kind=kOutput, calls=%fused_computation.43 | convolution fusion | flops 555745280 | bytes 1837056 | tf_op jit(solution)/shard_map/dot_general | solution.py:66
  50.6 2.8 %fusion.6 = f32[512,256]{1,0:T(8,128)S(1)} fusion(bf16[256,1024]{0,1:T(8,128)(2,1)S(1)} %bitcast.42, bf16[256,1024]{0,1:T(8,128)(2,1)S(1)} %bitcast.52), kind=kOutput, calls=%fused_computation.42 | convolution fusion | flops 555745280 | bytes 1835008 | tf_op jit(solution)/shard_map/dot_general | solution.py:66
  53.3 0.0 collective-permute-done.1
  53.3 4.8 %collective-permute-done = bf16[256,1024]{0,1:T(8,128)(2,1)S(1)} collective-permute-done((bf16[256,1024]{0,1:T(8,128)(2,1)S(1)}, bf16[256,1024]{0,1:T(8,128)(2,1)S(1)}, u32[]{:S(2)}, u32[]{:S(2)}) %collective-permute-start) | collective-permute-done | bytes 524320 | tf_op jit(solution)/shard_map/ppermute | solution.py:10
  58.1 4.8 %convolution_add_fusion.1 = f32[512,256]{1,0:T(8,128)} fusion(f32[512,256]{1,0:T(8,128)} %fusion.7, bf16[256,1024]{0,1:T(8,128)(2,1)S(1)} %collective-permute-done.1, bf16[256,1024]{0,1:T(8,128)(2,1)S(1)} %collective-permute-done, s32[512]{0:T(512)S(1)} %iota_add_fusion.2, s32[1024]{0:T(1024)S(1)} %iota_add_fusion.1, bf16[256,1024]{0,1:T(8,128)(2,1)S(1)} %bitcast.53), kind=kOutput, calls=%fused_computation.39 | convolution fusion | flops 555876352 | bytes 2365440 | tf_op jit(solution)/shard_map/dot_general | solution.py:66
  62.9 3.7 %convolution_add_fusion.3 = f32[512,256]{1,0:T(8,128)} fusion(f32[512,256]{1,0:T(8,128)S(1)} %fusion.6, bf16[256,1024]{0,1:T(8,128)(2,1)S(1)} %collective-permute-done.1, bf16[256,1024]{0,1:T(8,128)(2,1)S(1)} %collective-permute-done, s32[1024]{0:T(1024)S(1)} %iota_add_fusion.1, bf16[256,1024]{0,1:T(8,128)(2,1)S(1)} %bitcast.54), kind=kOutput, calls=%fused_computation.41 | convolution fusion | flops 555876352 | bytes 2363392 | tf_op jit(solution)/shard_map/dot_general | solution.py:66
  66.6 4.4 %convolution_add_fusion = f32[512,256]{1,0:T(8,128)S(1)} fusion(f32[512,256]{1,0:T(8,128)} %convolution_add_fusion.1, bf16[256,1024]{0,1:T(8,128)(2,1)S(1)} %collective-permute-done.3, bf16[256,1024]{0,1:T(8,128)(2,1)} %collective-permute-done.2, s32[512]{0:T(512)S(1)} %iota_add_fusion.2, s32[1024]{0:T(1024)S(1)} %iota_add_fusion, ...), kind=kOutput, calls=%fused_computation.38 | convolution fusion | flops 555876352 | bytes 2365440 | tf_op jit(solution)/shard_map/dot_general | solution.py:66
  71.0 4.0 %convolution_add_fusion.2 = f32[512,256]{1,0:T(8,128)S(1)} fusion(f32[512,256]{1,0:T(8,128)S(1)} %copy-done.3, bf16[256,1024]{0,1:T(8,128)(2,1)S(1)} %collective-permute-done.3, bf16[256,1024]{0,1:T(8,128)(2,1)} %collective-permute-done.2, s32[1024]{0:T(1024)S(1)} %iota_add_fusion, bf16[256,1024]{0,1:T(8,128)(2,1)S(1)} %bitcast.56), kind=kOutput, calls=%fused_computation.40 | convolution fusion | flops 555876352 | bytes 2363392 | tf_op jit(solution)/shard_map/dot_general | solution.py:66
  75.0 1.2 %maximum_add_fusion = f32[1024,256]{1,0:T(8,128)} fusion(f32[512,256]{1,0:T(8,128)S(1)} %convolution_add_fusion, f32[512,256]{1,0:T(8,128)S(1)} %convolution_add_fusion.2, f32[1024]{0:T(1024)S(1)} %copy-done.1, bf16[8,128,256]{2,1,0:T(8,128)(2,1)S(1)} %convolution_convert_fusion), kind=kLoop, calls=%fused_computation.44 | loop fusion | flops 1048576 | bytes 2625536 | tf_op jit(solution)/shard_map/add | solution.py:79
  (13 shorter events, 0.0 us)
Async XLA Ops:
  0.0 9.3 %copy-start = (bf16[16,16384]{1,0:T(8,128)(2,1)S(1)}, bf16[16,16384]{1,0:T(8,128)(2,1)}, u32[]{:S(2)}) copy-start(bf16[16,16384]{1,0:T(8,128)(2,1)} %param.4) | copy-start | bytes 1572868
  1.9 21.4 %all-to-all-start.1 = ((bf16[16,16,1024]{2,0,1:T(8,128)(2,1)}), bf16[16,16,1024]{2,0,1:T(8,128)(2,1)S(1)}, u32[]{:S(2)}, u32[]{:S(2)}) async-start(bf16[16,16,1024]{2,0,1:T(8,128)(2,1)} %bitcast.37), calls=%async_computation.1 | async-start | bytes 1048576 | tf_op jit(solution)/shard_map/all_to_all | solution.py:41
  9.3 18.6 %copy-start.2 = (s32[1024]{0:T(1024)S(1)}, s32[1024]{0:T(1024)}, u32[]{:S(2)}) copy-start(s32[1024]{0:T(1024)} %param.6) | copy-start | bytes 12292
  23.4 18.6 %all-to-all-start = ((bf16[16,16,1024]{2,0,1:T(8,128)(2,1)}), bf16[16,16,1024]{2,0,1:T(8,128)(2,1)S(1)}, u32[]{:S(2)}, u32[]{:S(2)}) async-start(bf16[16,16,1024]{2,0,1:T(8,128)(2,1)} %bitcast.38), calls=%async_computation | async-start | bytes 1048576 | tf_op jit(solution)/shard_map/all_to_all | solution.py:40
  28.4 25.0 %collective-permute-start.1 = (bf16[256,1024]{0,1:T(8,128)(2,1)S(1)}, bf16[256,1024]{0,1:T(8,128)(2,1)S(1)}, u32[]{:S(2)}, u32[]{:S(2)}) collective-permute-start(bf16[256,1024]{0,1:T(8,128)(2,1)S(1)} %bitcast.39), channel_id=1, source_target_pairs={{0,1},{1,2},{2,3},{3,4},{4,5},{5,6},{6,7},{7,8},{8,9},{9,10},{10,1... | collective-permute-start | bytes 1572872 | tf_op jit(solution)/shard_map/ppermute | solution.py:10
  31.9 34.7 %collective-permute-start.3 = (bf16[256,1024]{0,1:T(8,128)(2,1)S(1)}, bf16[256,1024]{0,1:T(8,128)(2,1)S(1)}, u32[]{:S(2)}, u32[]{:S(2)}) collective-permute-start(bf16[256,1024]{0,1:T(8,128)(2,1)S(1)} %bitcast.40), channel_id=1, source_target_pairs={{1,0},{2,1},{3,2},{4,3},{5,4},{6,5},{7,6},{8,7},{9,8},{10,9},{11,1... | collective-permute-start | bytes 1572872 | tf_op jit(solution)/shard_map/ppermute | solution.py:10
  42.4 15.7 %collective-permute-start = (bf16[256,1024]{0,1:T(8,128)(2,1)S(1)}, bf16[256,1024]{0,1:T(8,128)(2,1)S(1)}, u32[]{:S(2)}, u32[]{:S(2)}) collective-permute-start(bf16[256,1024]{0,1:T(8,128)(2,1)S(1)} %bitcast.49), channel_id=1, source_target_pairs={{0,1},{1,2},{2,3},{3,4},{4,5},{5,6},{6,7},{7,8},{8,9},{9,10},{10,1... | collective-permute-start | bytes 1572872 | tf_op jit(solution)/shard_map/ppermute | solution.py:10
  44.9 21.7 %collective-permute-start.2 = (bf16[256,1024]{0,1:T(8,128)(2,1)S(1)}, bf16[256,1024]{0,1:T(8,128)(2,1)}, u32[]{:S(2)}, u32[]{:S(2)}) collective-permute-start(bf16[256,1024]{0,1:T(8,128)(2,1)S(1)} %bitcast.50), channel_id=1, source_target_pairs={{1,0},{2,1},{3,2},{4,3},{5,4},{6,5},{7,6},{8,7},{9,8},{10,9},{11,1... | collective-permute-start | bytes 1572872 | tf_op jit(solution)/shard_map/ppermute | solution.py:10
  66.6 4.4 %copy-start.3 = (f32[512,256]{1,0:T(8,128)S(1)}, f32[512,256]{1,0:T(8,128)}, u32[]{:S(2)}) copy-start(f32[512,256]{1,0:T(8,128)} %convolution_add_fusion.3) | copy-start | bytes 1572868
  71.0 4.0 %copy-start.1 = (f32[1024]{0:T(1024)S(1)}, f32[1024]{0:T(1024)}, u32[]{:S(2)}) copy-start(f32[1024]{0:T(1024)} %param.7) | copy-start | bytes 12292
where the time goes:
time: 76.6 us; the launch traced here: 76.1 us
  waiting for transfers between devices  26.1 us (34%)
  matrix products  24 us (31%)
  starting transfers between devices  21.7 us (28%)
  local copies, waits for them, and re-layouts  2.97 us (4%)
  other arithmetic  1.21 us (2%)
    dot_general x6, matrix products, apply_rows(): lax.dot_general(weights, d_cols, (((1,), (1,)), ((), ())), preferred_elem...  23.3 us
    all_to_all x1, waiting for transfers between devices, on_device(): lax.all_to_all(innovations, 'obs', split_axis=1, concat_axis=0, tiled=True)  13.2 us
    ppermute x4, starting transfers between devices, shifted(): return lax.ppermute(shard, axis, pairs)  9.9 us
    all_to_all x1, waiting for transfers between devices, on_device(): lax.all_to_all(anomalies, 'obs', split_axis=1, concat_axis=0, tiled=True)  8.09 us
    all_to_all x1, starting transfers between devices, on_device(): lax.all_to_all(innovations, 'obs', split_axis=1, concat_axis=0, tiled=True)  7.35 us
    ppermute x4, waiting for transfers between devices, shifted(): return lax.ppermute(shard, axis, pairs)  4.78 us
    all_to_all x1, starting transfers between devices, on_device(): lax.all_to_all(anomalies, 'obs', split_axis=1, concat_axis=0, tiled=True)  4.5 us
    all_to_all x1, local copies, waits for them, and re-layouts, on_device(): lax.all_to_all(innovations, 'obs', split_axis=1, concat_axis=0, tiled=True)  1.93 us
  transfers between devices with their start and end apart: 6, of which 3 were waited for; matrix products, arithmetic and copies ran while one was open for 22% of the time, Pallas kernels for 0%

commit v1 on v0

--- a/solution.py
+++ b/solution.py
@@ -2,6 +2,13 @@
 import jax.numpy as jnp
 from jax import lax
 from jax.sharding import PartitionSpec as P
+
+
+def swap_blocks(array, name, split, join):
+    size = lax.axis_size(name)
+    blocks = jnp.stack(jnp.split(array, size, axis=split), axis=0)
+    blocks = lax.all_to_all(blocks, name, split_axis=0, concat_axis=0)
+    return jnp.concatenate(blocks, axis=join)
 
 
 def shifted(shard, axis, by):
@@ -38,7 +45,7 @@
 def on_device(anomalies, innovations, sort_order, obs_error):
     raw_y, raw_d = (
         lax.all_to_all(anomalies, "obs", split_axis=1, concat_axis=0, tiled=True),
-        lax.all_to_all(innovations, "obs", split_axis=1, concat_axis=0, tiled=True),
+        swap_blocks(innovations, "obs", 1, 0),
     )
     members = raw_y.shape[0]
     panel = raw_y.shape[1]

time: 76.6 us -> 97.8 us (1.28); the launches traced: 76.1 us -> 96.3 us
  local copies, waits for them, and re-layouts: 2.97 us -> 23.1 us
    unnamed x10 -> x25, local copies, waits for them, and re-layouts: 0.2 us -> 20.9 us
    all_to_all x1 -> x0, local copies, waits for them, and re-layouts: 1.93 us -> none  [on_device(): lax.all_to_all(innovations, 'obs', split_axis=1, concat_axis=0, tiled=True)]
    another operation x0 -> x1, local copies, waits for them, and re-layouts: none -> 1.37 us  [swap_blocks(): blocks = jnp.stack(jnp.split(array, size, axis=split), axis=0)]
  transfers between devices with their start and end apart: 6 -> 6, of which waited for: 3 -> 3; matrix products, arithmetic and copies ran while one was open for 22% -> 17% of each run, Pallas kernels for 0% -> 0%
where the time goes in v1:
time: 97.8 us; the launch traced here: 96.3 us
  waiting for transfers between devices  26.1 us (27%)
  matrix products  24 us (25%)
  local copies, waits for them, and re-layouts  23.1 us (24%)
  starting transfers between devices  21.7 us (22%)
  other arithmetic  1.21 us (1%)
    dot_general x6, matrix products, apply_rows(): lax.dot_general(weights, d_cols, (((1,), (1,)), ((), ())), preferred_elem...  23.3 us
    unnamed x25, local copies, waits for them, and re-layouts  20.9 us
    all_to_all x1, waiting for transfers between devices, swap_blocks(): blocks = lax.all_to_all(blocks, name, split_axis=0, concat_axis=0)  13.2 us
    ppermute x4, starting transfers between devices, shifted(): return lax.ppermute(shard, axis, pairs)  9.89 us
    all_to_all x1, waiting for transfers between devices, on_device(): lax.all_to_all(anomalies, 'obs', split_axis=1, concat_axis=0, tiled=True)  8.1 us
    all_to_all x1, starting transfers between devices, swap_blocks(): blocks = lax.all_to_all(blocks, name, split_axis=0, concat_axis=0)  7.35 us
    ppermute x4, waiting for transfers between devices, shifted(): return lax.ppermute(shard, axis, pairs)  4.78 us
    all_to_all x1, starting transfers between devices, on_device(): lax.all_to_all(anomalies, 'obs', split_axis=1, concat_axis=0, tiled=True)  4.5 us
  transfers between devices with their start and end apart: 6, of which 3 were waited for; matrix products, arithmetic and copies ran while one was open for 17% of the time, Pallas kernels for 0%

profile of v1, /device:TPU:1, one launch (start us, length us, event | category | flops | bytes accessed | tf_op | source)
XLA Modules:
  0.0 96.3 jit_solution(12035970150470161992)
XLA Ops:
  0.0 1.4 %constant_dynamic-update-slice_fusion.15 = bf16[16,16,1024]{2,1,0:T(8,128)(2,1)} fusion(bf16[16,16384]{1,0:T(8,128)(2,1)} %param.5), kind=kLoop, calls=%fused_computation.169 | loop fusion | bytes 65536
  1.4 1.4 %constant_dynamic-update-slice_fusion.14 = bf16[16,16,1024]{2,1,0:T(8,128)(2,1)} fusion(bf16[16,16,1024]{2,1,0:T(8,128)(2,1)} %constant_dynamic-update-slice_fusion.15, bf16[16,16384]{1,0:T(8,128)(2,1)} %param.5), kind=kLoop, calls=%fused_computation.168 | loop fusion | bytes 65536
  2.8 1.4 %constant_dynamic-update-slice_fusion.13 = bf16[16,16,1024]{2,1,0:T(8,128)(2,1)} fusion(bf16[16,16,1024]{2,1,0:T(8,128)(2,1)} %constant_dynamic-update-slice_fusion.14, bf16[16,16384]{1,0:T(8,128)(2,1)} %param.5), kind=kLoop, calls=%fused_computation.167 | loop fusion | bytes 65536
  4.2 1.4 %constant_dynamic-update-slice_fusion.12 = bf16[16,16,1024]{2,1,0:T(8,128)(2,1)} fusion(bf16[16,16,1024]{2,1,0:T(8,128)(2,1)} %constant_dynamic-update-slice_fusion.13, bf16[16,16384]{1,0:T(8,128)(2,1)} %param.5), kind=kLoop, calls=%fused_computation.166 | loop fusion | bytes 65536
  5.6 1.4 %constant_dynamic-update-slice_fusion.11 = bf16[16,16,1024]{2,1,0:T(8,128)(2,1)} fusion(bf16[16,16,1024]{2,1,0:T(8,128)(2,1)} %constant_dynamic-update-slice_fusion.12, bf16[16,16384]{1,0:T(8,128)(2,1)} %param.5), kind=kLoop, calls=%fused_computation.165 | loop fusion | bytes 65536
  6.9 1.4 %constant_dynamic-update-slice_fusion.10 = bf16[16,16,1024]{2,1,0:T(8,128)(2,1)} fusion(bf16[16,16,1024]{2,1,0:T(8,128)(2,1)} %constant_dynamic-update-slice_fusion.11, bf16[16,16384]{1,0:T(8,128)(2,1)} %param.5), kind=kLoop, calls=%fused_computation.164 | loop fusion | bytes 65536
  13.8 1.4 %constant_dynamic-update-slice_fusion.5 = bf16[16,16,1024]{2,1,0:T(8,128)(2,1)} fusion(bf16[16,16,1024]{2,1,0:T(8,128)(2,1)} %constant_dynamic-update-slice_fusion.6, bf16[16,16384]{1,0:T(8,128)(2,1)} %param.5), kind=kLoop, calls=%fused_computation.159 | loop fusion | bytes 65536
  16.6 1.4 %constant_dynamic-update-slice_fusion.3 = bf16[16,16,1024]{2,1,0:T(8,128)(2,1)} fusion(bf16[16,16,1024]{2,1,0:T(8,128)(2,1)} %constant_dynamic-update-slice_fusion.4, bf16[16,16384]{1,0:T(8,128)(2,1)} %param.5), kind=kLoop, calls=%fused_computation.157 | loop fusion | bytes 65536
  19.3 1.4 %constant_dynamic-update-slice_fusion.1 = bf16[16,16,1024]{2,1,0:T(8,128)(2,1)} fusion(bf16[16,16,1024]{2,1,0:T(8,128)(2,1)} %constant_dynamic-update-slice_fusion.2, bf16[16,16384]{1,0:T(8,128)(2,1)} %param.5), kind=kLoop, calls=%fused_computation.155 | loop fusion | bytes 65536
  22.0 7.3 %all-to-all-start.1 = ((bf16[16,16,1024]{2,1,0:T(8,128)(2,1)}), bf16[16,16,1024]{2,1,0:T(8,128)(2,1)S(1)}, u32[]{:S(2)}, u32[]{:S(2)}) async-start(bf16[16,16,1024]{2,1,0:T(8,128)(2,1)} %constant_dynamic-update-slice_fusion), calls=%async_computation.1 | async-start | bytes 1048576 | tf_op jit(solution)/shard_map/all_to_all | solution.py:10
  30.2 13.2 %all-to-all-done.1 = bf16[16,16,1024]{2,1,0:T(8,128)(2,1)S(1)} async-done(((bf16[16,16,1024]{2,1,0:T(8,128)(2,1)}), bf16[16,16,1024]{2,1,0:T(8,128)(2,1)S(1)}, u32[]{:S(2)}, u32[]{:S(2)}) %all-to-all-start.1) | async-done | bytes 524320 | tf_op jit(solution)/shard_map/all_to_all | solution.py:10
  43.5 4.5 %all-to-all-start = ((bf16[16,16,1024]{2,0,1:T(8,128)(2,1)}), bf16[16,16,1024]{2,0,1:T(8,128)(2,1)S(1)}, u32[]{:S(2)}, u32[]{:S(2)}) async-start(bf16[16,16,1024]{2,0,1:T(8,128)(2,1)} %bitcast.65), calls=%async_computation | async-start | bytes 1048576 | tf_op jit(solution)/shard_map/all_to_all | solution.py:47
  48.5 3.5 %collective-permute-start.1 = (bf16[256,1024]{0,1:T(8,128)(2,1)S(1)}, bf16[256,1024]{0,1:T(8,128)(2,1)S(1)}, u32[]{:S(2)}, u32[]{:S(2)}) collective-permute-start(bf16[256,1024]{0,1:T(8,128)(2,1)S(1)} %bitcast.66), channel_id=1, source_target_pairs={{0,1},{1,2},{2,3},{3,4},{4,5},{5,6},{6,7},{7,8},{8,9},{9,10},{10,1... | collective-permute-start | bytes 1572872 | tf_op jit(solution)/shard_map/ppermute | solution.py:17
  52.0 1.9 %collective-permute-start.3 = (bf16[256,1024]{0,1:T(8,128)(2,1)S(1)}, bf16[256,1024]{0,1:T(8,128)(2,1)S(1)}, u32[]{:S(2)}, u32[]{:S(2)}) collective-permute-start(bf16[256,1024]{0,1:T(8,128)(2,1)S(1)} %bitcast.67), channel_id=1, source_target_pairs={{1,0},{2,1},{3,2},{4,3},{5,4},{6,5},{7,6},{8,7},{9,8},{10,9},{11,1... | collective-permute-start | bytes 1572872 | tf_op jit(solution)/shard_map/ppermute | solution.py:17
  54.0 8.1 %all-to-all-done = bf16[16,16,1024]{2,0,1:T(8,128)(2,1)S(1)} async-done(((bf16[16,16,1024]{2,0,1:T(8,128)(2,1)}), bf16[16,16,1024]{2,0,1:T(8,128)(2,1)S(1)}, u32[]{:S(2)}, u32[]{:S(2)}) %all-to-all-start) | async-done | bytes 524320 | tf_op jit(solution)/shard_map/all_to_all | solution.py:47
  62.5 2.5 %collective-permute-start = (bf16[256,1024]{0,1:T(8,128)(2,1)S(1)}, bf16[256,1024]{0,1:T(8,128)(2,1)S(1)}, u32[]{:S(2)}, u32[]{:S(2)}) collective-permute-start(bf16[256,1024]{0,1:T(8,128)(2,1)S(1)} %bitcast.75), channel_id=1, source_target_pairs={{0,1},{1,2},{2,3},{3,4},{4,5},{5,6},{6,7},{7,8},{8,9},{9,10},{10,1... | collective-permute-start | bytes 1572872 | tf_op jit(solution)/shard_map/ppermute | solution.py:17
  65.0 1.9 %collective-permute-start.2 = (bf16[256,1024]{0,1:T(8,128)(2,1)S(1)}, bf16[256,1024]{0,1:T(8,128)(2,1)}, u32[]{:S(2)}, u32[]{:S(2)}) collective-permute-start(bf16[256,1024]{0,1:T(8,128)(2,1)S(1)} %bitcast.76), channel_id=1, source_target_pairs={{1,0},{2,1},{3,2},{4,3},{5,4},{6,5},{7,6},{8,7},{9,8},{10,9},{11,1... | collective-permute-start | bytes 1572872 | tf_op jit(solution)/shard_map/ppermute | solution.py:17
  66.9 3.8 %fusion.7 = f32[512,256]{1,0:T(8,128)} fusion(bf16[256,1024]{0,1:T(8,128)(2,1)S(1)} %bitcast.68, bf16[256,1024]{0,1:T(8,128)(2,1)S(1)} %bitcast.77, s32[512]{0:T(512)S(1)} %iota_add_fusion.2), kind=kOutput, calls=%fused_computation.43 | convolution fusion | flops 555745280 | bytes 1837056 | tf_op jit(solution)/shard_map/dot_general | solution.py:73
  70.7 2.8 %fusion.6 = f32[512,256]{1,0:T(8,128)S(1)} fusion(bf16[256,1024]{0,1:T(8,128)(2,1)S(1)} %bitcast.69, bf16[256,1024]{0,1:T(8,128)(2,1)S(1)} %bitcast.78), kind=kOutput, calls=%fused_computation.42 | convolution fusion | flops 555745280 | bytes 1835008 | tf_op jit(solution)/shard_map/dot_general | solution.py:73
  73.5 4.8 %collective-permute-done = bf16[256,1024]{0,1:T(8,128)(2,1)S(1)} collective-permute-done((bf16[256,1024]{0,1:T(8,128)(2,1)S(1)}, bf16[256,1024]{0,1:T(8,128)(2,1)S(1)}, u32[]{:S(2)}, u32[]{:S(2)}) %collective-permute-start) | collective-permute-done | bytes 524320 | tf_op jit(solution)/shard_map/ppermute | solution.py:17
  78.2 4.8 %convolution_add_fusion.1 = f32[512,256]{1,0:T(8,128)} fusion(f32[512,256]{1,0:T(8,128)} %fusion.7, bf16[256,1024]{0,1:T(8,128)(2,1)S(1)} %collective-permute-done.1, bf16[256,1024]{0,1:T(8,128)(2,1)S(1)} %collective-permute-done, s32[512]{0:T(512)S(1)} %iota_add_fusion.2, s32[1024]{0:T(1024)S(1)} %iota_add_fusion.1, bf16[256,1024]{0,1:T(8,128)(2,1)S(1)} %bitcast.79), kind=kOutput, calls=%fused_computation.39 | convolution fusion | flops 555876352 | bytes 2365440 | tf_op jit(solution)/shard_map/dot_general | solution.py:73
  83.0 3.7 %convolution_add_fusion.3 = f32[512,256]{1,0:T(8,128)} fusion(f32[512,256]{1,0:T(8,128)S(1)} %fusion.6, bf16[256,1024]{0,1:T(8,128)(2,1)S(1)} %collective-permute-done.1, bf16[256,1024]{0,1:T(8,128)(2,1)S(1)} %collective-permute-done, s32[1024]{0:T(1024)S(1)} %iota_add_fusion.1, bf16[256,1024]{0,1:T(8,128)(2,1)S(1)} %bitcast.80), kind=kOutput, calls=%fused_computation.41 | convolution fusion | flops 555876352 | bytes 2363392 | tf_op jit(solution)/shard_map/dot_general | solution.py:73
  86.7 4.4 %convolution_add_fusion = f32[512,256]{1,0:T(8,128)S(1)} fusion(f32[512,256]{1,0:T(8,128)} %convolution_add_fusion.1, bf16[256,1024]{0,1:T(8,128)(2,1)S(1)} %collective-permute-done.3, bf16[256,1024]{0,1:T(8,128)(2,1)} %collective-permute-done.2, s32[512]{0:T(512)S(1)} %iota_add_fusion.2, s32[1024]{0:T(1024)S(1)} %iota_add_fusion, ...), kind=kOutput, calls=%fused_computation.38 | convolution fusion | flops 555876352 | bytes 2365440 | tf_op jit(solution)/shard_map/dot_general | solution.py:73
  91.1 4.0 %convolution_add_fusion.2 = f32[512,256]{1,0:T(8,128)S(1)} fusion(f32[512,256]{1,0:T(8,128)S(1)} %copy-done.3, bf16[256,1024]{0,1:T(8,128)(2,1)S(1)} %collective-permute-done.3, bf16[256,1024]{0,1:T(8,128)(2,1)} %collective-permute-done.2, s32[1024]{0:T(1024)S(1)} %iota_add_fusion, bf16[256,1024]{0,1:T(8,128)(2,1)S(1)} %bitcast.82), kind=kOutput, calls=%fused_computation.40 | convolution fusion | flops 555876352 | bytes 2363392 | tf_op jit(solution)/shard_map/dot_general | solution.py:73
  (28 shorter events, 12.5 us)
Async XLA Ops:
  0.0 29.4 %copy-start = (bf16[16,16384]{1,0:T(8,128)(2,1)S(1)}, bf16[16,16384]{1,0:T(8,128)(2,1)}, u32[]{:S(2)}) copy-start(bf16[16,16384]{1,0:T(8,128)(2,1)} %param.4) | copy-start | bytes 1572868
  22.0 21.4 %all-to-all-start.1 = ((bf16[16,16,1024]{2,1,0:T(8,128)(2,1)}), bf16[16,16,1024]{2,1,0:T(8,128)(2,1)S(1)}, u32[]{:S(2)}, u32[]{:S(2)}) async-start(bf16[16,16,1024]{2,1,0:T(8,128)(2,1)} %constant_dynamic-update-slice_fusion), calls=%async_computation.1 | async-start | bytes 1048576 | tf_op jit(solution)/shard_map/all_to_all | solution.py:10
  29.4 18.6 %copy-start.2 = (s32[1024]{0:T(1024)S(1)}, s32[1024]{0:T(1024)}, u32[]{:S(2)}) copy-start(s32[1024]{0:T(1024)} %param.6) | copy-start | bytes 12292
  43.5 18.6 %all-to-all-start = ((bf16[16,16,1024]{2,0,1:T(8,128)(2,1)}), bf16[16,16,1024]{2,0,1:T(8,128)(2,1)S(1)}, u32[]{:S(2)}, u32[]{:S(2)}) async-start(bf16[16,16,1024]{2,0,1:T(8,128)(2,1)} %bitcast.65), calls=%async_computation | async-start | bytes 1048576 | tf_op jit(solution)/shard_map/all_to_all | solution.py:47
  48.5 25.0 %collective-permute-start.1 = (bf16[256,1024]{0,1:T(8,128)(2,1)S(1)}, bf16[256,1024]{0,1:T(8,128)(2,1)S(1)}, u32[]{:S(2)}, u32[]{:S(2)}) collective-permute-start(bf16[256,1024]{0,1:T(8,128)(2,1)S(1)} %bitcast.66), channel_id=1, source_target_pairs={{0,1},{1,2},{2,3},{3,4},{4,5},{5,6},{6,7},{7,8},{8,9},{9,10},{10,1... | collective-permute-start | bytes 1572872 | tf_op jit(solution)/shard_map/ppermute | solution.py:17
  52.0 34.7 %collective-permute-start.3 = (bf16[256,1024]{0,1:T(8,128)(2,1)S(1)}, bf16[256,1024]{0,1:T(8,128)(2,1)S(1)}, u32[]{:S(2)}, u32[]{:S(2)}) collective-permute-start(bf16[256,1024]{0,1:T(8,128)(2,1)S(1)} %bitcast.67), channel_id=1, source_target_pairs={{1,0},{2,1},{3,2},{4,3},{5,4},{6,5},{7,6},{8,7},{9,8},{10,9},{11,1... | collective-permute-start | bytes 1572872 | tf_op jit(solution)/shard_map/ppermute | solution.py:17
  62.5 15.7 %collective-permute-start = (bf16[256,1024]{0,1:T(8,128)(2,1)S(1)}, bf16[256,1024]{0,1:T(8,128)(2,1)S(1)}, u32[]{:S(2)}, u32[]{:S(2)}) collective-permute-start(bf16[256,1024]{0,1:T(8,128)(2,1)S(1)} %bitcast.75), channel_id=1, source_target_pairs={{0,1},{1,2},{2,3},{3,4},{4,5},{5,6},{6,7},{7,8},{8,9},{9,10},{10,1... | collective-permute-start | bytes 1572872 | tf_op jit(solution)/shard_map/ppermute | solution.py:17
  65.0 21.7 %collective-permute-start.2 = (bf16[256,1024]{0,1:T(8,128)(2,1)S(1)}, bf16[256,1024]{0,1:T(8,128)(2,1)}, u32[]{:S(2)}, u32[]{:S(2)}) collective-permute-start(bf16[256,1024]{0,1:T(8,128)(2,1)S(1)} %bitcast.76), channel_id=1, source_target_pairs={{1,0},{2,1},{3,2},{4,3},{5,4},{6,5},{7,6},{8,7},{9,8},{10,9},{11,1... | collective-permute-start | bytes 1572872 | tf_op jit(solution)/shard_map/ppermute | solution.py:17
  86.7 4.4 %copy-start.3 = (f32[512,256]{1,0:T(8,128)S(1)}, f32[512,256]{1,0:T(8,128)}, u32[]{:S(2)}) copy-start(f32[512,256]{1,0:T(8,128)} %convolution_add_fusion.3) | copy-start | bytes 1572868
  91.1 4.0 %copy-start.1 = (f32[1024]{0:T(1024)S(1)}, f32[1024]{0:T(1024)}, u32[]{:S(2)}) copy-start(f32[1024]{0:T(1024)} %param.7) | copy-start | bytes 12292
